TPU v7x, 32 devices: a whole 2x2x4 slice. The times are simulated.
32 devices in a mesh: seq: 8 (over z, y), tp: 4 (over x, core).
Axes of the slice: x: 2, y: 2, z: 4, core: 2. Of those that a mesh axis runs over, the one named last changes fastest.
Arguments:
- latent: bfloat16 [2048, 3072], P(('seq', 'tp')), may hold values from -6 to 6
- queries: bfloat16 [2048, 1536], P('seq', 'tp'), may hold values from -40 to 40
- key_vectors: bfloat16 [2048, 1536], P('seq', 'tp'), may hold values from -40 to 40
- value_vectors: bfloat16 [2048, 1536], P('seq', 'tp'), may hold values from -6 to 6
- proj_weight: bfloat16 [1536, 3072], P('tp'), may hold values from -0.15625 to 0.15625
- gate_scale: float32 [8, 3072], replicated, may hold values from -2 to 2
- text_length: int32 [8], replicated, may hold values from 64 to 128, as said below
- split_table: int32 [8, 1], replicated, may hold values from 64 to 256, as said below
Outputs:
- updated: bfloat16 [2048, 3072], P(('seq', 'tp'))
Inputs may be any that keep to these rules, and one draw needn't show every extreme that they name: `text_length`: some request has exactly 128 text tokens; text tokens are the first positions of a request. `split_table`: live slots of a device are its first ones; some request has an index of its group with all 256 slots live.
All inputs are finite; a program needn't handle non-finite values.
Results may differ from a plain program's by a relative error of at most 0.0075.
Values may be sent and summed in bfloat16 or wider, within the bound.
A program may use at most 64 MiB of HBM per device.

v0:
```python
import math

import jax
import jax.numpy as jnp
from jax import lax
from jax.sharding import PartitionSpec as P

HEAD_DIM = 128


def shortened(shard):
    return jax.tree.map(lambda a: a.astype(jnp.bfloat16) if a.dtype == jnp.float32 else a, shard)


def from_partner(block, axis, stride):
    count = lax.axis_size(axis)
    route = []
    for low in range(count):
        high = low | 1 << stride
        if high != low and high < count:
            route += [(low, high), (high, low)]
    return lax.ppermute(block, axis, route)


def hop_block(moving, bit_number):
    return jax.tree.map(
        lambda part, own: part.astype(own.dtype),
        from_partner(shortened(moving), "seq", bit_number),
        moving,
    )


def on_device(
    latent, queries, key_vectors, value_vectors, proj_weight, gate_scale, text_length, split_table
):
    group_size = split_table.shape[1]
    tokens = queries.shape[0]
    feature_width = queries.shape[1]
    head_count = feature_width // HEAD_DIM
    seq_index = lax.axis_index("seq")
    item_index = seq_index // group_size
    group_place = seq_index % group_size
    counts = lax.dynamic_index_in_dim(split_table, item_index, 0, keepdims=False)
    members = jnp.arange(group_size, dtype=jnp.int32)
    offset = jnp.sum(jnp.where(members < group_place, counts, 0))
    own_count = jnp.sum(jnp.where(members == group_place, counts, 0))
    slot_index = jnp.arange(tokens, dtype=jnp.int32)
    query_live = slot_index < own_count
    text_count = jnp.sum(
        jnp.where(jnp.arange(text_length.shape[0], dtype=jnp.int32) == item_index, text_length, 0)
    )
    image_mask = query_live & (offset + slot_index >= text_count)
    query_heads = queries.reshape(tokens, head_count, HEAD_DIM)
    score_scale = 1.0 / math.sqrt(HEAD_DIM)

    def absorb(softmax_carry, stacked, key_live):
        running_max, running_sum, running_acc = softmax_carry
        length = stacked.shape[1]
        key_heads = stacked[0].reshape(length, head_count, HEAD_DIM)
        value_heads = stacked[1].reshape(length, head_count, HEAD_DIM)
        scores = (
            jnp.einsum("qhd,khd->qhk", query_heads, key_heads, preferred_element_type=jnp.float32)
            * score_scale
        )
        scores = jnp.where(key_live[None, None, :], scores, -1e30)
        new_max = jnp.maximum(running_max, jnp.max(scores, axis=2))
        shrink = jnp.exp(running_max - new_max)
        weights = jnp.exp(scores - new_max[:, :, None]) * key_live[None, None, :].astype(
            jnp.float32
        )
        running_sum = running_sum * shrink + jnp.sum(weights, axis=2)
        running_acc = running_acc * shrink[:, :, None] + jnp.einsum(
            "qhk,khd->qhd",
            weights.astype(jnp.bfloat16),
            value_heads,
            preferred_element_type=jnp.float32,
        )
        return (new_max, running_sum, running_acc)

    stacked = jnp.stack([key_vectors, value_vectors])
    softmax_carry = (
        jnp.full((tokens, head_count), -1e30, jnp.float32),
        jnp.zeros((tokens, head_count), jnp.float32),
        jnp.zeros((tokens, head_count, HEAD_DIM), jnp.float32),
    )
    softmax_carry = absorb(softmax_carry, stacked, query_live)
    if group_size > 1:
        bit_total = group_size.bit_length() - 1

        def make_branch(bit_number):

            def branch(moving):
                return hop_block(moving, bit_number)

            return branch

        branch_list = [make_branch(bit_number) for bit_number in range(bit_total)]

        def cycle_step(step_index, loop_carry):
            inner_carry, moving = loop_carry
            trailing = jnp.int32(0)
            for bit_number in range(bit_total - 1):
                trailing = trailing + (step_index % (2 << bit_number) == 0).astype(jnp.int32)
            moving = lax.switch(trailing, branch_list, moving)
            anchor = jnp.bitwise_xor(group_place, jnp.bitwise_xor(step_index, step_index // 2))
            anchor_count = jnp.sum(jnp.where(members == anchor, counts, 0))
            return (absorb(inner_carry, moving, slot_index < anchor_count), moving)

        softmax_carry, moving = lax.fori_loop(1, group_size, cycle_step, (softmax_carry, stacked))
    running_max, running_sum, running_acc = softmax_carry
    attended = (
        (running_acc / running_sum[:, :, None]).reshape(tokens, feature_width).astype(jnp.bfloat16)
    )
    row_share = tokens // lax.axis_size("tp")
    projected = lax.psum_scatter(
        jnp.dot(attended, proj_weight, preferred_element_type=jnp.float32).astype(jnp.bfloat16),
        "tp",
        scatter_dimension=0,
        tiled=True,
    ).astype(jnp.float32)
    tp_first = lax.axis_index("tp") * row_share
    my_image = lax.dynamic_slice_in_dim(image_mask, tp_first, row_share, 0)
    gate_row = lax.dynamic_index_in_dim(gate_scale, item_index, 0, keepdims=False)
    residual_base = latent.astype(jnp.float32)
    return jnp.where(
        my_image[:, None], residual_base + gate_row[None, :] * projected, residual_base
    ).astype(jnp.bfloat16)


def solution(mesh):
    in_specs = (
        P(("seq", "tp"), None),
        P("seq", "tp"),
        P("seq", "tp"),
        P("seq", "tp"),
        P("tp", None),
        P(),
        P(),
        P(),
    )
    out_specs = P(("seq", "tp"), None)
    return jax.shard_map(
        on_device, mesh=mesh, in_specs=in_specs, out_specs=out_specs, check_vma=False
    )
```

profile of v0, /device:TPU:0, one launch (start us, length us, event | category | flops | bytes accessed | tf_op | source)
XLA Modules:
  0.0 54.6 jit_solution(13808135514961113906)
XLA Ops:
  6.5 0.0 copy-start
  6.5 0.0 reduce-scatter.2.cloned.1.call-start
  6.5 1.4 %constant_dynamic-slice_fusion.1 = s32[1,1]{0,1:T(1,128)} fusion(s32[8,1]{0,1:T(1,128)} %param.15, s32[]{:T(128)S(6)} %select_n.34), kind=kLoop, calls=%fused_computation.22 | loop fusion | bytes 12 | tf_op jit(solution)/shard_map/jit(dynamic_index_in_dim)/dynamic_slice | solution.py:43
  7.9 0.6 %iota_compare_fusion = (pred[256]{0:T(512)(128)(4,1)S(1)}, f32[256]{0:T(256)S(1)}) fusion(s32[]{:T(128)} %bitcast), kind=kLoop, calls=%fused_computation.19 | loop fusion | flops 512 | bytes 1284 | tf_op jit(solution)/shard_map/lt | solution.py:48
  8.6 1.1 %copy.13 = bf16[256,384]{0,1:T(8,128)(2,1)S(1)} copy(bf16[256,384]{1,0:T(8,128)(2,1)} %param.10) | data formatting | bytes 393216 | tf_op args[2]
  9.6 1.1 %copy.14 = bf16[256,384]{0,1:T(8,128)(2,1)S(1)} copy(bf16[256,384]{1,0:T(8,128)(2,1)} %param.9) | data formatting | bytes 393216 | tf_op args[1]
  10.7 0.3 fusion.14
  11.1 0.2 fusion.6
  11.3 1.1 %copy.17 = bf16[256,384]{0,1:T(8,128)(2,1)S(1)} copy(bf16[256,384]{1,0:T(8,128)(2,1)} %param.11) | data formatting | bytes 393216 | tf_op args[3]
  12.3 0.3 fusion.4
  12.6 0.0 copy-done
  12.6 0.0 copy-start.2
  12.6 0.0 copy-start.1
  12.7 2.2 %convolution_convert_fusion = bf16[256,3072]{1,0:T(8,128)(2,1)} fusion(bf16[256,384]{0,1:T(8,128)(2,1)S(1)} %bitcast.23, bf16[384,3072]{1,0:T(8,128)(2,1)S(1)} %copy-done), kind=kOutput, calls=%fused_computation | convolution fusion | flops 604766208 | bytes 4128768 | tf_op jit(solution)/shard_map/dot_general | solution.py:116
  14.8 0.0 reduce-scatter.2.cloned.1.call-update
  14.8 0.0 copy-done.2
  14.9 0.7 %fusion.11 = s32[]{:T(128)} fusion(s32[8]{0:T(128)S(1)} %copy-done.2, s32[]{:T(128)S(6)} %axis_index.23), kind=kLoop, calls=%fused_computation.20 | loop fusion | flops 23 | bytes 40 | tf_op jit(solution)/shard_map/reduce_sum | solution.py:49
  15.5 1.3 %compare_and_fusion = pred[256]{0:T(512)(128)(4,1)S(1)} fusion(s32[]{:T(128)} %fusion.11, s32[]{:T(128)} %bitcast), kind=kLoop, calls=%fused_computation.17 | loop fusion | flops 768 | bytes 264 | tf_op jit(solution)/shard_map/and | solution.py:52
  16.8 0.1 dynamic_slice.12
  16.9 0.9 %constant_dynamic-slice_fusion = f32[1,3072]{1,0:T(1,128)S(1)} fusion(f32[8,3072]{1,0:T(8,128)} %param.13, s32[]{:T(128)S(6)} %select_n.34), kind=kLoop, calls=%fused_computation.21 | loop fusion | bytes 24580 | tf_op jit(solution)/shard_map/jit(dynamic_index_in_dim)/dynamic_slice | solution.py:123
  17.8 28.0 %reduce-scatter.2.cloned.1.call-done = bf16[64,3072]{1,0:T(8,128)(2,1)} async-done(((bf16[256,3072]{1,0:T(8,128)(2,1)}), bf16[64,3072]{1,0:T(8,128)(2,1)}) %reduce-scatter.2.cloned.1.call-update) | async-done | bytes 393232 | tf_op jit(solution)/shard_map/reduce_scatter | solution.py:115
  45.8 0.0 copy-done.1
  45.8 1.9 %fusion.5 = bf16[64,3072]{1,0:T(8,128)(2,1)} fusion(bf16[64,3072]{1,0:T(8,128)(2,1)} %reduce-scatter.2.cloned.1.call-done, bf16[64,3072]{1,0:T(8,128)(2,1)S(1)} %copy-done.1, f32[3072]{0:T(1024)S(1)} %bitcast.25, pred[64]{0:T(512)(128)(4,1)S(1)} %dynamic_slice.12), kind=kLoop, calls=%fused_computation.9 | loop fusion | flops 1179648 | bytes 1192000 | tf_op jit(solution)/shard_map/convert_element_type | solution.py:127
  (2 shorter events, 0.0 us)
Async XLA Ops:
  6.5 6.1 %copy-start = (bf16[384,3072]{1,0:T(8,128)(2,1)S(1)}, bf16[384,3072]{1,0:T(8,128)(2,1)}, u32[]{:S(2)}) copy-start(bf16[384,3072]{1,0:T(8,128)(2,1)} %param.12) | copy-start | bytes 7077892
  6.5 39.3 %reduce-scatter.2.cloned.1.call-start = ((), (), s32[]{:S(2)}) async-start(), calls=%async_computation.1 | async-start | bytes 1966080 | tf_op jit(solution)/shard_map/reduce_scatter | solution.py:115
  12.6 2.2 %copy-start.2 = (s32[8]{0:T(128)S(1)}, s32[8]{0:T(128)}, u32[]{:S(2)}) copy-start(s32[8]{0:T(128)} %param.14) | copy-start | bytes 100
  12.6 33.2 %copy-start.1 = (bf16[64,3072]{1,0:T(8,128)(2,1)S(1)}, bf16[64,3072]{1,0:T(8,128)(2,1)}, u32[]{:S(2)}) copy-start(bf16[64,3072]{1,0:T(8,128)(2,1)} %param.8) | copy-start | bytes 1179652
Sparse Core Ops, SparseCore 0:
  15.0 30.8 reduce-scatter.1
where the time goes:
time: 54.9 us; the launch traced here: 54.6 us
  waiting for transfers between devices  28.1 us (51%)
  between operations  13.5 us (25%)
  local copies, waits for them, and re-layouts  5.58 us (10%)
  other arithmetic  4.71 us (9%)
  matrix products  2.78 us (5%)
    reduce_scatter x1, waiting for transfers between devices, on_device(): lax.psum_scatter(jnp.dot(attended, proj_weight, preferred_element_type=jn...  28 us
    unnamed x9, local copies, waits for them, and re-layouts  3.21 us
    dot_general x1, matrix products, on_device(): jnp.dot(attended, proj_weight, preferred_element_type=jnp.float32)  2.16 us
    convert_element_type x1, other arithmetic, on_device(): return jnp.where(my_image[:, None], residual_base + gate_row[None, :] * p...  1.94 us
    dynamic_slice x1, local copies, waits for them, and re-layouts, on_device(): lax.dynamic_index_in_dim(split_table, item_index, 0, keepdims=False)  1.39 us
    and x1, other arithmetic, on_device(): image_mask = query_live & (offset + slot_index >= text_count)  1.29 us
  transfers between devices with their start and end apart: 1, of which 1 were waited for; matrix products, arithmetic and copies ran while one was open for 5% of the time, Pallas kernels for 0%

commit v1 on v0

--- a/solution.py
+++ b/solution.py
@@ -1,11 +1,212 @@
+import functools
 import math
 
 import jax
 import jax.numpy as jnp
 from jax import lax
+from jax.experimental import pallas as pl
+from jax.experimental.pallas import tpu as pltpu
 from jax.sharding import PartitionSpec as P
 
 HEAD_DIM = 128
+LEAST_TEXT = 64
+CHUNKS = 6
+MESH = pl.DeviceIdType.MESH
+
+
+def local_kernel(
+    latent, queries, key_vectors, value_vectors, proj_weight, gate_scale, text_length, split_table,
+    out,
+    q_buf, k_buf, v_buf, w_buf, latent_buf, gate_buf, text_buf, table_buf,
+    attended, mate_send, mate_recv, kept, far_send, far_recv, near_send, near_recv, own,
+    q_sem, kv_sem, w_sem, small_sem,
+    mate_sems, far_sems, near_sems,
+):
+    seq, tp = lax.axis_index("seq"), lax.axis_index("tp")
+    core = lax.rem(tp, 2)
+    mate = tp + 1 - 2 * core
+    far = lax.rem(tp + 2, 4)
+    far_mate = lax.rem(mate + 2, 4)
+    tokens, width = q_buf.shape
+    block = tokens // 4
+    heads = width // HEAD_DIM
+    columns = w_buf.shape[2]
+
+    barrier = pltpu.get_barrier_semaphore()
+    for other in (mate, far):
+        pl.semaphore_signal(barrier, inc=1, device_id=(seq, other), device_id_type=MESH)
+
+    q_copies = []
+    for place, owner in enumerate((far_mate, far, mate, tp)):
+        q_copies.append(
+            pltpu.make_async_copy(
+                queries.at[pl.ds(pl.multiple_of(owner * block, block), block)],
+                q_buf.at[pl.ds(place * block, block)],
+                q_sem.at[place],
+            )
+        )
+    k_copy = pltpu.make_async_copy(key_vectors, k_buf, kv_sem.at[0])
+    v_copy = pltpu.make_async_copy(value_vectors, v_buf, kv_sem.at[1])
+    table_copy = pltpu.make_async_copy(split_table, table_buf, small_sem.at[0])
+    text_copy = pltpu.make_async_copy(text_length, text_buf, small_sem.at[1])
+    gate_copy = pltpu.make_async_copy(gate_scale, gate_buf, small_sem.at[2])
+    latent_copy = pltpu.make_async_copy(latent, latent_buf, small_sem.at[3])
+    w_copies = [
+        pltpu.make_async_copy(proj_weight.at[:, pl.ds(i * columns, columns)], w_buf.at[i], w_sem.at[i])
+        for i in range(CHUNKS)
+    ]
+    for copy in (table_copy, k_copy, *q_copies, v_copy, *w_copies, text_copy, gate_copy, latent_copy):
+        copy.start()
+
+    def remote(source, target, sems, i, other):
+        return pltpu.make_async_remote_copy(
+            src_ref=source.at[i],
+            dst_ref=target.at[i],
+            send_sem=sems.at[0, i],
+            recv_sem=sems.at[1, i],
+            device_id=(seq, other),
+            device_id_type=MESH,
+        )
+
+    to_mate = [remote(mate_send, mate_recv, mate_sems, i, mate) for i in range(CHUNKS)]
+    to_far = [remote(far_send, far_recv, far_sems, i, far) for i in range(CHUNKS)]
+    to_owner = [remote(near_send, near_recv, near_sems, i, mate) for i in range(CHUNKS)]
+
+    table_copy.wait()
+    count = table_buf[seq]
+    key_live = lax.broadcasted_iota(jnp.int32, (1, tokens), 1) < count
+    score_scale = 1.0 / math.sqrt(HEAD_DIM)
+
+    def attend(first):
+        rows = pl.ds(first, 2 * block)
+        for head in range(heads):
+            part = pl.ds(head * HEAD_DIM, HEAD_DIM)
+            scores = lax.dot_general(
+                q_buf[rows, part], k_buf[:, part], (((1,), (1,)), ((), ())),
+                preferred_element_type=jnp.float32,
+            )
+            scores = jnp.where(key_live, scores * score_scale, -1e30)
+            top = jnp.max(scores, axis=1, keepdims=True)
+            weights = jnp.exp(scores - top)
+            total = jnp.sum(weights, axis=1, keepdims=True)
+            summed = jnp.dot(
+                weights.astype(jnp.bfloat16), v_buf[:, part], preferred_element_type=jnp.float32
+            )
+            attended[rows, part] = (summed / total).astype(jnp.bfloat16)
+
+    k_copy.wait()
+    for copy in q_copies:
+        copy.wait()
+    v_copy.wait()
+    attend(0)
+
+    for i in range(CHUNKS + 1):
+        if i < CHUNKS:
+            w_copies[i].wait()
+            share = jnp.dot(
+                attended[pl.ds(0, 2 * block), :], w_buf[i], preferred_element_type=jnp.float32
+            )
+            mate_send[i] = share[:block].astype(jnp.bfloat16)
+            kept[i] = share[block:]
+            if i == 0:
+                pl.semaphore_wait(barrier, 2)
+
+            @pl.when(tp != 3)
+            def _():
+                to_mate[i].start()
+
+        if i >= 1:
+            j = i - 1
+
+            @pl.when(tp != 2)
+            def _():
+                to_mate[j].wait_recv()
+                far_send[j] = (kept[j] + mate_recv[j].astype(jnp.float32)).astype(jnp.bfloat16)
+                to_far[j].start()
+
+    attend(2 * block)
+    for i in range(CHUNKS):
+        share = jnp.dot(
+            attended[pl.ds(2 * block, 2 * block), :], w_buf[i], preferred_element_type=jnp.float32
+        )
+        near_send[i] = share[:block].astype(jnp.bfloat16)
+        own[i] = share[block:]
+
+        @pl.when(tp != 1)
+        def _():
+            to_owner[i].start()
+
+    text_copy.wait()
+    gate_copy.wait()
+    latent_copy.wait()
+    text = text_buf[seq]
+    position = tp * block + lax.broadcasted_iota(jnp.int32, (block, 1), 0)
+    image = (position >= text) & (position < count)
+
+    @pl.when(tp == 0)
+    def _():
+        out[...] = latent_buf[...]
+
+    @pl.when(tp != 0)
+    def _():
+        for i in range(CHUNKS):
+            part = pl.ds(i * columns, columns)
+            to_owner[i].wait_recv()
+            projected = own[i] + near_recv[i].astype(jnp.float32)
+            to_far[i].wait_recv()
+            projected = projected + far_recv[i].astype(jnp.float32)
+            base = latent_buf[:, part].astype(jnp.float32)
+            gate = gate_buf[pl.ds(seq, 1), part]
+            out[:, part] = jnp.where(image, base + gate * projected, base).astype(jnp.bfloat16)
+
+    for copies, idle in ((to_mate, 3), (to_far, 2), (to_owner, 1)):
+
+        @pl.when(tp != idle)
+        def _():
+            for copy in copies:
+                copy.wait_send()
+
+
+def on_device_local(
+    latent, queries, key_vectors, value_vectors, proj_weight, gate_scale, text_length, split_table
+):
+    tokens, width = queries.shape
+    model = proj_weight.shape[1]
+    block, columns = tokens // 4, model // CHUNKS
+    in_hbm = pl.BlockSpec(memory_space=pltpu.HBM)
+    blocks16 = pltpu.VMEM((CHUNKS, block, columns), jnp.bfloat16)
+    blocks32 = pltpu.VMEM((CHUNKS, block, columns), jnp.float32)
+    return pl.pallas_call(
+        local_kernel,
+        out_shape=jax.ShapeDtypeStruct(latent.shape, latent.dtype),
+        in_specs=[in_hbm] * 8,
+        out_specs=pl.BlockSpec(memory_space=pltpu.VMEM),
+        scratch_shapes=[
+            pltpu.VMEM((tokens, width), jnp.bfloat16),
+            pltpu.VMEM((tokens, width), jnp.bfloat16),
+            pltpu.VMEM((tokens, width), jnp.bfloat16),
+            pltpu.VMEM((CHUNKS, width, columns), jnp.bfloat16),
+            pltpu.VMEM(latent.shape, jnp.bfloat16),
+            pltpu.VMEM(gate_scale.shape, jnp.float32),
+            pltpu.SMEM(text_length.shape, jnp.int32),
+            pltpu.SMEM((split_table.size,), jnp.int32),
+            pltpu.VMEM((tokens, width), jnp.bfloat16),
+            blocks16, blocks16, blocks32, blocks16, blocks16, blocks16, blocks16, blocks32,
+            pltpu.SemaphoreType.DMA((4,)),
+            pltpu.SemaphoreType.DMA((2,)),
+            pltpu.SemaphoreType.DMA((CHUNKS,)),
+            pltpu.SemaphoreType.DMA((4,)),
+            pltpu.SemaphoreType.DMA((2, CHUNKS)),
+            pltpu.SemaphoreType.DMA((2, CHUNKS)),
+            pltpu.SemaphoreType.DMA((2, CHUNKS)),
+        ],
+        compiler_params=pltpu.CompilerParams(
+            collective_id=0, has_side_effects=True, vmem_limit_bytes=64 * 2**20
+        ),
+        cost_estimate=pl.CostEstimate(
+            flops=2 * tokens * width * (model + 2 * tokens), bytes_accessed=4 * 2**20, transcendentals=0
+        ),
+    )(latent, queries, key_vectors, value_vectors, proj_weight, gate_scale, text_length, split_table.reshape(-1))
 
 
 def shortened(shard):
@@ -139,6 +340,16 @@
         P(),
     )
     out_specs = P(("seq", "tp"), None)
-    return jax.shard_map(
-        on_device, mesh=mesh, in_specs=in_specs, out_specs=out_specs, check_vma=False
-    )
+
+    def updated(
+        latent, queries, key_vectors, value_vectors, proj_weight, gate_scale, text_length, split_table
+    ):
+        tokens = queries.shape[0] // mesh.shape["seq"]
+        whole_request = split_table.shape[1] == 1
+        text_first = mesh.shape["tp"] == 4 and tokens // 4 <= LEAST_TEXT
+        return jax.shard_map(
+            on_device_local if whole_request and text_first else on_device,
+            mesh=mesh, in_specs=in_specs, out_specs=out_specs, check_vma=False,
+        )(latent, queries, key_vectors, value_vectors, proj_weight, gate_scale, text_length, split_table)
+
+    return updated

time: 54.9 us -> 17.1 us (0.31)
  the two profiles are of different devices: /device:TPU:0 before, /device:TPU:27 now
where the time goes in v1:
time: 17.1 us; the launch traced here: 16.9 us
  Pallas kernels  15.2 us (89%)
  local copies, waits for them, and re-layouts  1.77 us (10%)
    pallas_call x1, Pallas kernels, on_device_local(): pl.pallas_call(local_kernel, out_shape=jax.ShapeDtypeStruct(latent.shape,...  15.2 us
    unnamed x1, local copies, waits for them, and re-layouts  1.77 us

profile of v1, /device:TPU:27, one launch (start us, length us, event | category | flops | bytes accessed | tf_op | source)
XLA Modules:
  0.0 16.9 jit_solution(17032672192050328945)
XLA Ops:
  0.0 15.2 %shard_map.82 = bf16[64,3072]{1,0:T(8,128)(2,1)} custom-call(bf16[64,3072]{1,0:T(8,128)(2,1)} %latent.1, bf16[256,384]{1,0:T(8,128)(2,1)} %queries.1, bf16[256,384]{1,0:T(8,128)(2,1)} %key_vectors.1, bf16[256,384]{1,0:T(8,128)(2,1)} %value_vectors.1, bf16[384,3072]{1,0:T(8,128)(2,1)} %proj_weight.1, f32[8,3072]{1,0:T(8,128)} %gate_scale.1, s32[8]{0:T(128)} %text_length.1, ...), custom_call_target="tpu_custom_call" | custom-call | flops 704643072 | bytes 4194304 | tf_op jit(solution)/shard_map/pallas_call | solution.py:179
  15.2 1.8 %copy.10 = bf16[64,3072]{1,0:T(8,128)(2,1)} copy(bf16[64,3072]{1,0:T(8,128)(2,1)} %shard_map.82) | data formatting | bytes 786432

commit v2 on v1

--- a/solution.py
+++ b/solution.py
@@ -16,10 +16,10 @@
 
 def local_kernel(
     latent, queries, key_vectors, value_vectors, proj_weight, gate_scale, text_length, split_table,
-    out,
+    base, arrived,
     q_buf, k_buf, v_buf, w_buf, latent_buf, gate_buf, text_buf, table_buf,
-    attended, mate_send, mate_recv, kept, far_send, far_recv, near_send, near_recv, own,
-    q_sem, kv_sem, w_sem, small_sem,
+    attended, mate_send, mate_recv, kept, far_send, near_send, near_recv, own,
+    q_sem, kv_sem, w_sem, small_sem, base_sem,
     mate_sems, far_sems, near_sems,
 ):
     seq, tp = lax.axis_index("seq"), lax.axis_index("tp")
@@ -61,16 +61,20 @@
     def remote(source, target, sems, i, other):
         return pltpu.make_async_remote_copy(
             src_ref=source.at[i],
-            dst_ref=target.at[i],
+            dst_ref=target,
             send_sem=sems.at[0, i],
             recv_sem=sems.at[1, i],
             device_id=(seq, other),
             device_id_type=MESH,
         )
 
-    to_mate = [remote(mate_send, mate_recv, mate_sems, i, mate) for i in range(CHUNKS)]
-    to_far = [remote(far_send, far_recv, far_sems, i, far) for i in range(CHUNKS)]
-    to_owner = [remote(near_send, near_recv, near_sems, i, mate) for i in range(CHUNKS)]
+    parts = [pl.ds(i * columns, columns) for i in range(CHUNKS)]
+    to_mate = [remote(mate_send, mate_recv.at[i], mate_sems, i, mate) for i in range(CHUNKS)]
+    to_far = [remote(far_send, arrived.at[:, parts[i]], far_sems, i, far) for i in range(CHUNKS)]
+    to_owner = [remote(near_send, near_recv.at[i], near_sems, i, mate) for i in range(CHUNKS)]
+    base_copies = [
+        pltpu.make_async_copy(own.at[i], base.at[:, parts[i]], base_sem.at[i]) for i in range(CHUNKS)
+    ]
 
     table_copy.wait()
     count = table_buf[seq]
@@ -99,7 +103,16 @@
         copy.wait()
     v_copy.wait()
     attend(0)
-
+    text_copy.wait()
+    gate_copy.wait()
+    latent_copy.wait()
+    text = text_buf[seq]
+
+    def image(owner):
+        position = owner * block + lax.broadcasted_iota(jnp.int32, (block, 1), 0)
+        return (position >= text) & (position < count)
+
+    far_image = image(far)
     for i in range(CHUNKS + 1):
         if i < CHUNKS:
             w_copies[i].wait()
@@ -121,7 +134,9 @@
             @pl.when(tp != 2)
             def _():
                 to_mate[j].wait_recv()
-                far_send[j] = (kept[j] + mate_recv[j].astype(jnp.float32)).astype(jnp.bfloat16)
+                summed = kept[j] + mate_recv[j].astype(jnp.float32)
+                gated = gate_buf[pl.ds(seq, 1), parts[j]] * summed
+                far_send[j] = jnp.where(far_image, gated, 0.0).astype(jnp.bfloat16)
                 to_far[j].start()
 
     attend(2 * block)
@@ -136,29 +151,36 @@
         def _():
             to_owner[i].start()
 
-    text_copy.wait()
-    gate_copy.wait()
-    latent_copy.wait()
-    text = text_buf[seq]
-    position = tp * block + lax.broadcasted_iota(jnp.int32, (block, 1), 0)
-    image = (position >= text) & (position < count)
+    near_image = image(tp)
 
     @pl.when(tp == 0)
     def _():
-        out[...] = latent_buf[...]
+        near_recv[...] = jnp.zeros_like(near_recv)
+        zero_copies = [
+            pltpu.make_async_copy(near_recv.at[i], arrived.at[:, parts[i]], far_sems.at[1, i])
+            for i in range(CHUNKS)
+        ]
+        for i in range(CHUNKS):
+            zero_copies[i].start()
+            own[i] = latent_buf[:, parts[i]].astype(jnp.float32)
+            base_copies[i].start()
+        for copy in zero_copies:
+            copy.wait()
 
     @pl.when(tp != 0)
     def _():
         for i in range(CHUNKS):
-            part = pl.ds(i * columns, columns)
             to_owner[i].wait_recv()
             projected = own[i] + near_recv[i].astype(jnp.float32)
+            residual = latent_buf[:, parts[i]].astype(jnp.float32)
+            gate = gate_buf[pl.ds(seq, 1), parts[i]]
+            own[i] = jnp.where(near_image, residual + gate * projected, residual)
+            base_copies[i].start()
+        for i in range(CHUNKS):
             to_far[i].wait_recv()
-            projected = projected + far_recv[i].astype(jnp.float32)
-            base = latent_buf[:, part].astype(jnp.float32)
-            gate = gate_buf[pl.ds(seq, 1), part]
-            out[:, part] = jnp.where(image, base + gate * projected, base).astype(jnp.bfloat16)
-
+
+    for copy in base_copies:
+        copy.wait()
     for copies, idle in ((to_mate, 3), (to_far, 2), (to_owner, 1)):
 
         @pl.when(tp != idle)
@@ -176,11 +198,14 @@
     in_hbm = pl.BlockSpec(memory_space=pltpu.HBM)
     blocks16 = pltpu.VMEM((CHUNKS, block, columns), jnp.bfloat16)
     blocks32 = pltpu.VMEM((CHUNKS, block, columns), jnp.float32)
-    return pl.pallas_call(
+    base, arrived = pl.pallas_call(
         local_kernel,
-        out_shape=jax.ShapeDtypeStruct(latent.shape, latent.dtype),
+        out_shape=(
+            jax.ShapeDtypeStruct(latent.shape, jnp.float32),
+            jax.ShapeDtypeStruct(latent.shape, jnp.bfloat16),
+        ),
         in_specs=[in_hbm] * 8,
-        out_specs=pl.BlockSpec(memory_space=pltpu.VMEM),
+        out_specs=(in_hbm, in_hbm),
         scratch_shapes=[
             pltpu.VMEM((tokens, width), jnp.bfloat16),
             pltpu.VMEM((tokens, width), jnp.bfloat16),
@@ -191,11 +216,12 @@
             pltpu.SMEM(text_length.shape, jnp.int32),
             pltpu.SMEM((split_table.size,), jnp.int32),
             pltpu.VMEM((tokens, width), jnp.bfloat16),
-            blocks16, blocks16, blocks32, blocks16, blocks16, blocks16, blocks16, blocks32,
+            blocks16, blocks16, blocks32, blocks16, blocks16, blocks16, blocks32,
             pltpu.SemaphoreType.DMA((4,)),
             pltpu.SemaphoreType.DMA((2,)),
             pltpu.SemaphoreType.DMA((CHUNKS,)),
             pltpu.SemaphoreType.DMA((4,)),
+            pltpu.SemaphoreType.DMA((CHUNKS,)),
             pltpu.SemaphoreType.DMA((2, CHUNKS)),
             pltpu.SemaphoreType.DMA((2, CHUNKS)),
             pltpu.SemaphoreType.DMA((2, CHUNKS)),
@@ -207,6 +233,7 @@
             flops=2 * tokens * width * (model + 2 * tokens), bytes_accessed=4 * 2**20, transcendentals=0
         ),
     )(latent, queries, key_vectors, value_vectors, proj_weight, gate_scale, text_length, split_table.reshape(-1))
+    return (base + arrived.astype(jnp.float32)).astype(jnp.bfloat16)
 
 
 def shortened(shard):

time: 17.1 us -> 16.8 us (0.982)
  other arithmetic: 0 us -> 2.05 us
  local copies, waits for them, and re-layouts: 1.77 us -> 0 us
  Pallas kernels: 15.2 us -> 14.6 us
    convert_element_type x0 -> x1, other arithmetic: none -> 2.05 us  [on_device_local(): return (base + arrived.astype(jnp.float32)).astype(jnp.bfloat16)]
    unnamed x1 -> x0, local copies, waits for them, and re-layouts: 1.77 us -> none
    pallas_call x1, Pallas kernels: 15.2 us -> 14.6 us  [on_device_local(): pl.pallas_call(local_kernel, out_shape=(jax.ShapeDtypeStruct(latent.shape...]
where the time goes in v2:
time: 16.8 us; the launch traced here: 16.7 us
  Pallas kernels  14.6 us (87%)
  other arithmetic  2.05 us (12%)
    pallas_call x1, Pallas kernels, on_device_local(): pl.pallas_call(local_kernel, out_shape=(jax.ShapeDtypeStruct(latent.shape...  14.6 us
    convert_element_type x1, other arithmetic, on_device_local(): return (base + arrived.astype(jnp.float32)).astype(jnp.bfloat16)  2.05 us

profile of v2, /device:TPU:27, one launch (start us, length us, event | category | flops | bytes accessed | tf_op | source)
XLA Modules:
  0.0 16.7 jit_solution(11524690433300354388)
XLA Ops:
  0.0 14.6 %shard_map.82 = (f32[64,3072]{1,0:T(8,128)}, bf16[64,3072]{1,0:T(8,128)(2,1)}) custom-call(bf16[64,3072]{1,0:T(8,128)(2,1)} %latent.1, bf16[256,384]{1,0:T(8,128)(2,1)} %queries.1, bf16[256,384]{1,0:T(8,128)(2,1)} %key_vectors.1, bf16[256,384]{1,0:T(8,128)(2,1)} %value_vectors.1, bf16[384,3072]{1,0:T(8,128)(2,1)} %proj_weight.1, f32[8,3072]{1,0:T(8,128)} %gate_scale.1, ...), custom_call_target="tpu_custom_call" | custom-call | flops 704643072 | bytes 4194304 | tf_op jit(solution)/shard_map/pallas_call | solution.py:201
  14.6 2.0 %add_convert_fusion = bf16[64,3072]{1,0:T(8,128)(2,1)} fusion(f32[64,3072]{1,0:T(8,128)} %get-tuple-element.7, bf16[64,3072]{1,0:T(8,128)(2,1)} %get-tuple-element.8), kind=kLoop, calls=%fused_computation | loop fusion | flops 589824 | bytes 1572864 | tf_op jit(solution)/shard_map/convert_element_type | solution.py:236

commit v3 on v2

--- a/solution.py
+++ b/solution.py
@@ -10,7 +10,8 @@
 
 HEAD_DIM = 128
 LEAST_TEXT = 64
-CHUNKS = 6
+CHUNKS = 12
+AHEAD = 4
 MESH = pl.DeviceIdType.MESH
 
 
@@ -46,7 +47,14 @@
             )
         )
     k_copy = pltpu.make_async_copy(key_vectors, k_buf, kv_sem.at[0])
-    v_copy = pltpu.make_async_copy(value_vectors, v_buf, kv_sem.at[1])
+    v_copies = [
+        pltpu.make_async_copy(
+            value_vectors.at[:, pl.ds(head * HEAD_DIM, HEAD_DIM)],
+            v_buf.at[:, pl.ds(2 * head * HEAD_DIM, HEAD_DIM)],
+            kv_sem.at[1 + head],
+        )
+        for head in range(heads)
+    ]
     table_copy = pltpu.make_async_copy(split_table, table_buf, small_sem.at[0])
     text_copy = pltpu.make_async_copy(text_length, text_buf, small_sem.at[1])
     gate_copy = pltpu.make_async_copy(gate_scale, gate_buf, small_sem.at[2])
@@ -55,7 +63,7 @@
         pltpu.make_async_copy(proj_weight.at[:, pl.ds(i * columns, columns)], w_buf.at[i], w_sem.at[i])
         for i in range(CHUNKS)
     ]
-    for copy in (table_copy, k_copy, *q_copies, v_copy, *w_copies, text_copy, gate_copy, latent_copy):
+    for copy in (table_copy, k_copy, *q_copies, *v_copies, *w_copies, text_copy, gate_copy, latent_copy):
         copy.start()
 
     def remote(source, target, sems, i, other):
@@ -76,32 +84,41 @@
         pltpu.make_async_copy(own.at[i], base.at[:, parts[i]], base_sem.at[i]) for i in range(CHUNKS)
     ]
 
+    for head in range(heads):
+        v_buf[:, pl.ds((2 * head + 1) * HEAD_DIM, HEAD_DIM)] = jnp.ones((tokens, HEAD_DIM), jnp.bfloat16)
+
     table_copy.wait()
     count = table_buf[seq]
     key_live = lax.broadcasted_iota(jnp.int32, (1, tokens), 1) < count
-    score_scale = 1.0 / math.sqrt(HEAD_DIM)
+    score_scale = math.log2(math.e) / math.sqrt(HEAD_DIM)
 
     def attend(first):
         rows = pl.ds(first, 2 * block)
-        for head in range(heads):
-            part = pl.ds(head * HEAD_DIM, HEAD_DIM)
-            scores = lax.dot_general(
+        columns_of = [pl.ds(head * HEAD_DIM, HEAD_DIM) for head in range(heads)]
+        scores = [
+            lax.dot_general(
                 q_buf[rows, part], k_buf[:, part], (((1,), (1,)), ((), ())),
                 preferred_element_type=jnp.float32,
             )
-            scores = jnp.where(key_live, scores * score_scale, -1e30)
-            top = jnp.max(scores, axis=1, keepdims=True)
-            weights = jnp.exp(scores - top)
-            total = jnp.sum(weights, axis=1, keepdims=True)
-            summed = jnp.dot(
-                weights.astype(jnp.bfloat16), v_buf[:, part], preferred_element_type=jnp.float32
+            for part in columns_of
+        ]
+        scores = [jnp.where(key_live, one * score_scale, -1e30) for one in scores]
+        weights = [jnp.exp2(one - jnp.max(one, axis=1, keepdims=True)) for one in scores]
+        summed = [
+            jnp.dot(
+                one.astype(jnp.bfloat16), v_buf[:, pl.ds(2 * head * HEAD_DIM, 2 * HEAD_DIM)],
+                preferred_element_type=jnp.float32,
             )
-            attended[rows, part] = (summed / total).astype(jnp.bfloat16)
+            for head, one in enumerate(weights)
+        ]
+        for part, one in zip(columns_of, summed):
+            attended[rows, part] = (one[:, :HEAD_DIM] / one[:, HEAD_DIM:]).astype(jnp.bfloat16)
 
     k_copy.wait()
     for copy in q_copies:
         copy.wait()
-    v_copy.wait()
+    for copy in v_copies:
+        copy.wait()
     attend(0)
     text_copy.wait()
     gate_copy.wait()
@@ -113,7 +130,7 @@
         return (position >= text) & (position < count)
 
     far_image = image(far)
-    for i in range(CHUNKS + 1):
+    for i in range(CHUNKS + AHEAD):
         if i < CHUNKS:
             w_copies[i].wait()
             share = jnp.dot(
@@ -128,8 +145,8 @@
             def _():
                 to_mate[i].start()
 
-        if i >= 1:
-            j = i - 1
+        if i >= AHEAD:
+            j = i - AHEAD
 
             @pl.when(tp != 2)
             def _():
@@ -209,7 +226,7 @@
         scratch_shapes=[
             pltpu.VMEM((tokens, width), jnp.bfloat16),
             pltpu.VMEM((tokens, width), jnp.bfloat16),
-            pltpu.VMEM((tokens, width), jnp.bfloat16),
+            pltpu.VMEM((tokens, 2 * width), jnp.bfloat16),
             pltpu.VMEM((CHUNKS, width, columns), jnp.bfloat16),
             pltpu.VMEM(latent.shape, jnp.bfloat16),
             pltpu.VMEM(gate_scale.shape, jnp.float32),
@@ -218,7 +235,7 @@
             pltpu.VMEM((tokens, width), jnp.bfloat16),
             blocks16, blocks16, blocks32, blocks16, blocks16, blocks16, blocks32,
             pltpu.SemaphoreType.DMA((4,)),
-            pltpu.SemaphoreType.DMA((2,)),
+            pltpu.SemaphoreType.DMA((1 + width // HEAD_DIM,)),
             pltpu.SemaphoreType.DMA((CHUNKS,)),
             pltpu.SemaphoreType.DMA((4,)),
             pltpu.SemaphoreType.DMA((CHUNKS,)),

time: 16.8 us -> 16.9 us (level)
  no operation moved by 1% of the time
where the time goes in v3:
time: 16.9 us; the launch traced here: 16.7 us
  Pallas kernels  14.6 us (86%)
  other arithmetic  2.05 us (12%)
    pallas_call x1, Pallas kernels, on_device_local(): pl.pallas_call(local_kernel, out_shape=(jax.ShapeDtypeStruct(latent.shape...  14.6 us
    convert_element_type x1, other arithmetic, on_device_local(): return (base + arrived.astype(jnp.float32)).astype(jnp.bfloat16)  2.05 us

profile of v3, /device:TPU:27, one launch (start us, length us, event | category | flops | bytes accessed | tf_op | source)
XLA Modules:
  0.0 16.7 jit_solution(5131688714255487978)
XLA Ops:
  0.0 14.6 %shard_map.82 = (f32[64,3072]{1,0:T(8,128)}, bf16[64,3072]{1,0:T(8,128)(2,1)}) custom-call(bf16[64,3072]{1,0:T(8,128)(2,1)} %latent.1, bf16[256,384]{1,0:T(8,128)(2,1)} %queries.1, bf16[256,384]{1,0:T(8,128)(2,1)} %key_vectors.1, bf16[256,384]{1,0:T(8,128)(2,1)} %value_vectors.1, bf16[384,3072]{1,0:T(8,128)(2,1)} %proj_weight.1, f32[8,3072]{1,0:T(8,128)} %gate_scale.1, ...), custom_call_target="tpu_custom_call" | custom-call | flops 704643072 | bytes 4194304 | tf_op jit(solution)/shard_map/pallas_call | solution.py:218
  14.7 2.0 %add_convert_fusion = bf16[64,3072]{1,0:T(8,128)(2,1)} fusion(f32[64,3072]{1,0:T(8,128)} %get-tuple-element.7, bf16[64,3072]{1,0:T(8,128)(2,1)} %get-tuple-element.8), kind=kLoop, calls=%fused_computation | loop fusion | flops 589824 | bytes 1572864 | tf_op jit(solution)/shard_map/convert_element_type | solution.py:253

commit v4 on v3

--- a/solution.py
+++ b/solution.py
@@ -11,7 +11,7 @@
 HEAD_DIM = 128
 LEAST_TEXT = 64
 CHUNKS = 12
-AHEAD = 4
+AHEAD = 3
 MESH = pl.DeviceIdType.MESH
 
 
@@ -92,8 +92,8 @@
     key_live = lax.broadcasted_iota(jnp.int32, (1, tokens), 1) < count
     score_scale = math.log2(math.e) / math.sqrt(HEAD_DIM)
 
-    def attend(first):
-        rows = pl.ds(first, 2 * block)
+    def attend(first, length):
+        rows = pl.ds(first, length)
         columns_of = [pl.ds(head * HEAD_DIM, HEAD_DIM) for head in range(heads)]
         scores = [
             lax.dot_general(
@@ -119,7 +119,25 @@
         copy.wait()
     for copy in v_copies:
         copy.wait()
-    attend(0)
+    def send_to_mate(i, share):
+        mate_send[i] = share.astype(jnp.bfloat16)
+
+        @pl.when(tp != 3)
+        def _():
+            to_mate[i].start()
+
+    def product(first, length, i):
+        return jnp.dot(
+            attended[pl.ds(first, length), :], w_buf[i], preferred_element_type=jnp.float32
+        )
+
+    attend(0, block)
+    pl.semaphore_wait(barrier, 2)
+    for i in range(AHEAD):
+        w_copies[i].wait()
+        send_to_mate(i, product(0, block, i))
+    attend(block, block)
+
     text_copy.wait()
     gate_copy.wait()
     latent_copy.wait()
@@ -130,33 +148,26 @@
         return (position >= text) & (position < count)
 
     far_image = image(far)
-    for i in range(CHUNKS + AHEAD):
-        if i < CHUNKS:
-            w_copies[i].wait()
-            share = jnp.dot(
-                attended[pl.ds(0, 2 * block), :], w_buf[i], preferred_element_type=jnp.float32
-            )
-            mate_send[i] = share[:block].astype(jnp.bfloat16)
-            kept[i] = share[block:]
-            if i == 0:
-                pl.semaphore_wait(barrier, 2)
-
-            @pl.when(tp != 3)
-            def _():
-                to_mate[i].start()
-
-        if i >= AHEAD:
-            j = i - AHEAD
-
-            @pl.when(tp != 2)
-            def _():
-                to_mate[j].wait_recv()
-                summed = kept[j] + mate_recv[j].astype(jnp.float32)
-                gated = gate_buf[pl.ds(seq, 1), parts[j]] * summed
-                far_send[j] = jnp.where(far_image, gated, 0.0).astype(jnp.bfloat16)
-                to_far[j].start()
-
-    attend(2 * block)
+    for i in range(CHUNKS):
+        if i < AHEAD:
+            kept[i] = product(block, block, i)
+
+        @pl.when(tp != 2)
+        def _():
+            to_mate[i].wait_recv()
+            summed = kept[i] + mate_recv[i].astype(jnp.float32)
+            gated = gate_buf[pl.ds(seq, 1), parts[i]] * summed
+            far_send[i] = jnp.where(far_image, gated, 0.0).astype(jnp.bfloat16)
+            to_far[i].start()
+
+        later = i + AHEAD
+        if later < CHUNKS:
+            w_copies[later].wait()
+            share = product(0, 2 * block, later)
+            kept[later] = share[block:]
+            send_to_mate(later, share[:block])
+
+    attend(2 * block, 2 * block)
     for i in range(CHUNKS):
         share = jnp.dot(
             attended[pl.ds(2 * block, 2 * block), :], w_buf[i], preferred_element_type=jnp.float32

time: 16.9 us -> 16.8 us (level)
  no operation moved by 1% of the time
where the time goes in v4:
time: 16.8 us; the launch traced here: 16.5 us
  Pallas kernels  14.5 us (86%)
  other arithmetic  2.05 us (12%)
    pallas_call x1, Pallas kernels, on_device_local(): pl.pallas_call(local_kernel, out_shape=(jax.ShapeDtypeStruct(latent.shape...  14.5 us
    convert_element_type x1, other arithmetic, on_device_local(): return (base + arrived.astype(jnp.float32)).astype(jnp.bfloat16)  2.05 us

profile of v4, /device:TPU:27, one launch (start us, length us, event | category | flops | bytes accessed | tf_op | source)
XLA Modules:
  0.0 16.5 jit_solution(10976341411321580688)
XLA Ops:
  0.0 14.5 %shard_map.82 = (f32[64,3072]{1,0:T(8,128)}, bf16[64,3072]{1,0:T(8,128)(2,1)}) custom-call(bf16[64,3072]{1,0:T(8,128)(2,1)} %latent.1, bf16[256,384]{1,0:T(8,128)(2,1)} %queries.1, bf16[256,384]{1,0:T(8,128)(2,1)} %key_vectors.1, bf16[256,384]{1,0:T(8,128)(2,1)} %value_vectors.1, bf16[384,3072]{1,0:T(8,128)(2,1)} %proj_weight.1, f32[8,3072]{1,0:T(8,128)} %gate_scale.1, ...), custom_call_target="tpu_custom_call" | custom-call | flops 704643072 | bytes 4194304 | tf_op jit(solution)/shard_map/pallas_call | solution.py:229
  14.5 2.0 %add_convert_fusion = bf16[64,3072]{1,0:T(8,128)(2,1)} fusion(f32[64,3072]{1,0:T(8,128)} %get-tuple-element.7, bf16[64,3072]{1,0:T(8,128)(2,1)} %get-tuple-element.8), kind=kLoop, calls=%fused_computation | loop fusion | flops 589824 | bytes 1572864 | tf_op jit(solution)/shard_map/convert_element_type | solution.py:264

commit v5 on v4

--- a/solution.py
+++ b/solution.py
@@ -12,6 +12,7 @@
 LEAST_TEXT = 64
 CHUNKS = 12
 AHEAD = 3
+STRIPS = 2
 MESH = pl.DeviceIdType.MESH
 
 
@@ -215,6 +216,31 @@
         def _():
             for copy in copies:
                 copy.wait_send()
+
+
+def add_kernel(base, arrived, out, base_buf, arrived_buf, out_buf, sems):
+    step = out.shape[0] // STRIPS
+    rows = [pl.ds(i * step, step) for i in range(STRIPS)]
+    loads = [
+        (
+            pltpu.make_async_copy(arrived.at[part], arrived_buf.at[part], sems.at[0, i]),
+            pltpu.make_async_copy(base.at[part], base_buf.at[part], sems.at[1, i]),
+        )
+        for i, part in enumerate(rows)
+    ]
+    stores = [
+        pltpu.make_async_copy(out_buf.at[part], out.at[part], sems.at[2, i]) for i, part in enumerate(rows)
+    ]
+    for pair in loads:
+        for copy in pair:
+            copy.start()
+    for part, pair, store in zip(rows, loads, stores):
+        for copy in pair:
+            copy.wait()
+        out_buf[part] = (base_buf[part] + arrived_buf[part].astype(jnp.float32)).astype(jnp.bfloat16)
+        store.start()
+    for store in stores:
+        store.wait()
 
 
 def on_device_local(
@@ -261,7 +287,20 @@
             flops=2 * tokens * width * (model + 2 * tokens), bytes_accessed=4 * 2**20, transcendentals=0
         ),
     )(latent, queries, key_vectors, value_vectors, proj_weight, gate_scale, text_length, split_table.reshape(-1))
-    return (base + arrived.astype(jnp.float32)).astype(jnp.bfloat16)
+    return pl.pallas_call(
+        add_kernel,
+        out_shape=jax.ShapeDtypeStruct(latent.shape, latent.dtype),
+        in_specs=[in_hbm] * 2,
+        out_specs=in_hbm,
+        scratch_shapes=[
+            pltpu.VMEM(latent.shape, jnp.float32),
+            pltpu.VMEM(latent.shape, jnp.bfloat16),
+            pltpu.VMEM(latent.shape, jnp.bfloat16),
+            pltpu.SemaphoreType.DMA((3, STRIPS)),
+        ],
+        compiler_params=pltpu.CompilerParams(vmem_limit_bytes=64 * 2**20),
+        cost_estimate=pl.CostEstimate(flops=latent.size, bytes_accessed=8 * latent.size, transcendentals=0),
+    )(base, arrived)
 
 
 def shortened(shard):

time: 16.8 us -> 16.8 us (level)
  other arithmetic: 2.05 us -> 0 us
  Pallas kernels: 14.5 us -> 16.5 us
    convert_element_type x1 -> x0, other arithmetic: 2.05 us -> none  [on_device_local(): return (base + arrived.astype(jnp.float32)).astype(jnp.bfloat16)]
    pallas_call x0 -> x1, Pallas kernels: none -> 2.04 us  [on_device_local(): pl.pallas_call(add_kernel, out_shape=jax.ShapeDtypeStruct(latent.shape, l...]
where the time goes in v5:
time: 16.8 us; the launch traced here: 16.5 us
  Pallas kernels  16.5 us (98%)
    pallas_call x1, Pallas kernels, on_device_local(): pl.pallas_call(local_kernel, out_shape=(jax.ShapeDtypeStruct(latent.shape...  14.5 us
    pallas_call x1, Pallas kernels, on_device_local(): pl.pallas_call(add_kernel, out_shape=jax.ShapeDtypeStruct(latent.shape, l...  2.04 us

profile of v5, /device:TPU:27, one launch (start us, length us, event | category | flops | bytes accessed | tf_op | source)
XLA Modules:
  0.0 16.5 jit_solution(4537033897485679154)
XLA Ops:
  0.0 14.5 %shard_map.82 = (f32[64,3072]{1,0:T(8,128)}, bf16[64,3072]{1,0:T(8,128)(2,1)}) custom-call(bf16[64,3072]{1,0:T(8,128)(2,1)} %latent.1, bf16[256,384]{1,0:T(8,128)(2,1)} %queries.1, bf16[256,384]{1,0:T(8,128)(2,1)} %key_vectors.1, bf16[256,384]{1,0:T(8,128)(2,1)} %value_vectors.1, bf16[384,3072]{1,0:T(8,128)(2,1)} %proj_weight.1, f32[8,3072]{1,0:T(8,128)} %gate_scale.1, ...), custom_call_target="tpu_custom_call" | custom-call | flops 704643072 | bytes 4194304 | tf_op jit(solution)/shard_map/pallas_call | solution.py:255
  14.5 2.0 %shard_map.83 = bf16[64,3072]{1,0:T(8,128)(2,1)} custom-call(f32[64,3072]{1,0:T(8,128)} %get-tuple-element.7.base, bf16[64,3072]{1,0:T(8,128)(2,1)} %get-tuple-element.8.arrived), custom_call_target="tpu_custom_call" | custom-call | flops 196608 | bytes 1572864 | tf_op jit(solution)/shard_map/pallas_call | solution.py:290

commit v6 on v4

--- a/solution.py
+++ b/solution.py
@@ -63,7 +63,7 @@
         pltpu.make_async_copy(proj_weight.at[:, pl.ds(i * columns, columns)], w_buf.at[i], w_sem.at[i])
         for i in range(CHUNKS)
     ]
-    for copy in (table_copy, k_copy, *q_copies, *v_copies, *w_copies, text_copy, gate_copy, latent_copy):
+    for copy in (table_copy, *q_copies, k_copy, *v_copies, text_copy, gate_copy, *w_copies, latent_copy):
         copy.start()
 
     def remote(source, target, sems, i, other):
@@ -140,7 +140,6 @@
 
     text_copy.wait()
     gate_copy.wait()
-    latent_copy.wait()
     text = text_buf[seq]
 
     def image(owner):
@@ -179,6 +178,7 @@
         def _():
             to_owner[i].start()
 
+    latent_copy.wait()
     near_image = image(tp)
 
     @pl.when(tp == 0)

time: 16.8 us -> 16.8 us (level)
  no operation moved by 1% of the time
where the time goes in v6:
time: 16.8 us; the launch traced here: 16.5 us
  Pallas kernels  14.5 us (86%)
  other arithmetic  2.05 us (12%)
    pallas_call x1, Pallas kernels, on_device_local(): pl.pallas_call(local_kernel, out_shape=(jax.ShapeDtypeStruct(latent.shape...  14.5 us
    convert_element_type x1, other arithmetic, on_device_local(): return (base + arrived.astype(jnp.float32)).astype(jnp.bfloat16)  2.05 us

profile of v6, /device:TPU:27, one launch (start us, length us, event | category | flops | bytes accessed | tf_op | source)
XLA Modules:
  0.0 16.5 jit_solution(16125927749041416428)
XLA Ops:
  0.0 14.5 %shard_map.82 = (f32[64,3072]{1,0:T(8,128)}, bf16[64,3072]{1,0:T(8,128)(2,1)}) custom-call(bf16[64,3072]{1,0:T(8,128)(2,1)} %latent.1, bf16[256,384]{1,0:T(8,128)(2,1)} %queries.1, bf16[256,384]{1,0:T(8,128)(2,1)} %key_vectors.1, bf16[256,384]{1,0:T(8,128)(2,1)} %value_vectors.1, bf16[384,3072]{1,0:T(8,128)(2,1)} %proj_weight.1, f32[8,3072]{1,0:T(8,128)} %gate_scale.1, ...), custom_call_target="tpu_custom_call" | custom-call | flops 704643072 | bytes 4194304 | tf_op jit(solution)/shard_map/pallas_call | solution.py:229
  14.5 2.0 %add_convert_fusion = bf16[64,3072]{1,0:T(8,128)(2,1)} fusion(f32[64,3072]{1,0:T(8,128)} %get-tuple-element.7, bf16[64,3072]{1,0:T(8,128)(2,1)} %get-tuple-element.8), kind=kLoop, calls=%fused_computation | loop fusion | flops 589824 | bytes 1572864 | tf_op jit(solution)/shard_map/convert_element_type | solution.py:264

commit v7 on v6

--- a/solution.py
+++ b/solution.py
@@ -10,8 +10,8 @@
 
 HEAD_DIM = 128
 LEAST_TEXT = 64
-CHUNKS = 12
-AHEAD = 3
+CHUNKS = 6
+AHEAD = 2
 MESH = pl.DeviceIdType.MESH
 
 

time: 16.8 us -> 16.2 us (0.964)
  Pallas kernels: 14.5 us -> 14 us
    pallas_call x1, Pallas kernels: 14.5 us -> 14 us  [on_device_local(): pl.pallas_call(local_kernel, out_shape=(jax.ShapeDtypeStruct(latent.shape...]
where the time goes in v7:
time: 16.2 us; the launch traced here: 16.1 us
  Pallas kernels  14 us (86%)
  other arithmetic  2.05 us (13%)
    pallas_call x1, Pallas kernels, on_device_local(): pl.pallas_call(local_kernel, out_shape=(jax.ShapeDtypeStruct(latent.shape...  14 us
    convert_element_type x1, other arithmetic, on_device_local(): return (base + arrived.astype(jnp.float32)).astype(jnp.bfloat16)  2.05 us

profile of v7, /device:TPU:27, one launch (start us, length us, event | category | flops | bytes accessed | tf_op | source)
XLA Modules:
  0.0 16.1 jit_solution(1851029219910977762)
XLA Ops:
  0.0 14.0 %shard_map.82 = (f32[64,3072]{1,0:T(8,128)}, bf16[64,3072]{1,0:T(8,128)(2,1)}) custom-call(bf16[64,3072]{1,0:T(8,128)(2,1)} %latent.1, bf16[256,384]{1,0:T(8,128)(2,1)} %queries.1, bf16[256,384]{1,0:T(8,128)(2,1)} %key_vectors.1, bf16[256,384]{1,0:T(8,128)(2,1)} %value_vectors.1, bf16[384,3072]{1,0:T(8,128)(2,1)} %proj_weight.1, f32[8,3072]{1,0:T(8,128)} %gate_scale.1, ...), custom_call_target="tpu_custom_call" | custom-call | flops 704643072 | bytes 4194304 | tf_op jit(solution)/shard_map/pallas_call | solution.py:229
  14.0 2.0 %add_convert_fusion = bf16[64,3072]{1,0:T(8,128)(2,1)} fusion(f32[64,3072]{1,0:T(8,128)} %get-tuple-element.7, bf16[64,3072]{1,0:T(8,128)(2,1)} %get-tuple-element.8), kind=kLoop, calls=%fused_computation | loop fusion | flops 589824 | bytes 1572864 | tf_op jit(solution)/shard_map/convert_element_type | solution.py:264

commit v8 on v7

--- a/solution.py
+++ b/solution.py
@@ -10,7 +10,7 @@
 
 HEAD_DIM = 128
 LEAST_TEXT = 64
-CHUNKS = 6
+CHUNKS = 4
 AHEAD = 2
 MESH = pl.DeviceIdType.MESH
 

time: 16.2 us -> 16.1 us (level)
    pallas_call x1, Pallas kernels: 14 us -> 13.9 us  [on_device_local(): pl.pallas_call(local_kernel, out_shape=(jax.ShapeDtypeStruct(latent.shape...]
where the time goes in v8:
time: 16.1 us; the launch traced here: 15.9 us
  Pallas kernels  13.9 us (86%)
  other arithmetic  2.05 us (13%)
    pallas_call x1, Pallas kernels, on_device_local(): pl.pallas_call(local_kernel, out_shape=(jax.ShapeDtypeStruct(latent.shape...  13.9 us
    convert_element_type x1, other arithmetic, on_device_local(): return (base + arrived.astype(jnp.float32)).astype(jnp.bfloat16)  2.05 us

profile of v8, /device:TPU:27, one launch (start us, length us, event | category | flops | bytes accessed | tf_op | source)
XLA Modules:
  0.0 15.9 jit_solution(17741161130777539083)
XLA Ops:
  0.0 13.9 %shard_map.82 = (f32[64,3072]{1,0:T(8,128)}, bf16[64,3072]{1,0:T(8,128)(2,1)}) custom-call(bf16[64,3072]{1,0:T(8,128)(2,1)} %latent.1, bf16[256,384]{1,0:T(8,128)(2,1)} %queries.1, bf16[256,384]{1,0:T(8,128)(2,1)} %key_vectors.1, bf16[256,384]{1,0:T(8,128)(2,1)} %value_vectors.1, bf16[384,3072]{1,0:T(8,128)(2,1)} %proj_weight.1, f32[8,3072]{1,0:T(8,128)} %gate_scale.1, ...), custom_call_target="tpu_custom_call" | custom-call | flops 704643072 | bytes 4194304 | tf_op jit(solution)/shard_map/pallas_call | solution.py:229
  13.9 2.0 %add_convert_fusion = bf16[64,3072]{1,0:T(8,128)(2,1)} fusion(f32[64,3072]{1,0:T(8,128)} %get-tuple-element.7, bf16[64,3072]{1,0:T(8,128)(2,1)} %get-tuple-element.8), kind=kLoop, calls=%fused_computation | loop fusion | flops 589824 | bytes 1572864 | tf_op jit(solution)/shard_map/convert_element_type | solution.py:264
